TPU v7x, 32 devices: a whole 2x2x4 slice. The times are simulated.
32 devices in a mesh: rows: 4 (over z), segment: 4 (over y, x), tm: 2 (over core).
Axes of the slice: x: 2, y: 2, z: 4, core: 2. Of those that a mesh axis runs over, the one named last changes fastest.
Arguments:
- latents: bfloat16 [4, 8, 8, 128, 128], P(None, 'tm', 'rows'), may hold values from -40 to 40
- conv_first: bfloat16 [4, 3, 3, 3, 128, 128], P('segment'), may hold values from -0.109375 to 0.109375
- conv_second: bfloat16 [4, 3, 3, 3, 128, 128], P('segment'), may hold values from -0.109375 to 0.109375
- gain_first: bfloat16 [4, 128], P('segment'), may hold values from 0.099609375 to 1.8984375
- bias_first: bfloat16 [4, 128], P('segment'), may hold values from -1 to 1
- gain_second: bfloat16 [4, 128], P('segment'), may hold values from 0.099609375 to 1.8984375
- bias_second: bfloat16 [4, 128], P('segment'), may hold values from -1 to 1
Outputs:
- decoded: bfloat16 [4, 8, 8, 128, 128], P('segment', 'tm', 'rows')
All inputs are finite; a program needn't handle non-finite values.
Results may differ from a plain program's by a relative error of at most 0.022.
Values may be sent and summed in bfloat16 or wider, within the bound.
A program may use at most 64 MiB of HBM per device.

v0:
```python
import jax
import jax.numpy as jnp
from jax import lax
from jax.sharding import PartitionSpec as P

GROUPS = 32


EPS = 1e-06


def passed_along(value, axis, steps):
    count = lax.axis_size(axis)
    initial, last = (max(0, -steps), min(count, count - steps))
    return lax.ppermute(value, axis, [(source, source + steps) for source in range(initial, last)])


def padded_2(block, sides, width):
    for axis, dim in sides:
        count = lax.axis_size(axis)
        forward = [(i, i + 1) for i in range(count - 1)]
        backward = [(target, source) for source, target in forward]
        low = lax.ppermute(
            lax.slice_in_dim(block, block.shape[dim] - width, None, axis=dim), axis, forward
        )
        high = lax.ppermute(lax.slice_in_dim(block, 0, width, axis=dim), axis, backward)
        block = jnp.concatenate([low, block, high], axis=dim)
    return block


def normalize(values, norm_gain, norm_bias):
    frames, rows_here, columns, channels = values.shape
    width_group = channels // GROUPS
    grouped = values.astype(jnp.float32).reshape(frames, rows_here, columns, GROUPS, width_group)
    totals = lax.psum(
        (jnp.sum(grouped, axis=(0, 1, 2, 4)), jnp.sum(grouped * grouped, axis=(0, 1, 2, 4))), "rows"
    )
    members = frames * rows_here * lax.axis_size("rows") * columns * width_group
    average = totals[0] / members
    squares = totals[1] / members
    inverse = lax.rsqrt(squares - average * average + EPS)
    scaled = (grouped - average[:, None]) * inverse[:, None]
    scaled = scaled.reshape(values.shape) * norm_gain.astype(jnp.float32) + norm_bias.astype(
        jnp.float32
    )
    return jax.nn.silu(scaled).astype(jnp.bfloat16)


def convolve(active, kernel):
    previous = passed_along(active[-2:], "tm", 1)
    extended = jnp.concatenate([previous, active], axis=0)
    padded = padded_2(extended, (("rows", 1),), 1)
    padded = jnp.pad(padded, ((0, 0), (0, 0), (1, 1), (0, 0)))
    result = lax.conv_general_dilated(
        padded[None],
        kernel,
        (1, 1, 1),
        "VALID",
        dimension_numbers=("NDHWC", "DHWIO", "NDHWC"),
        preferred_element_type=jnp.float32,
    )
    return result[0]


def residual_block(values, params):
    first, second, gain_one, bias_one, gain_two, bias_two = params
    active = normalize(values, gain_one, bias_one)
    hidden = convolve(active, first).astype(jnp.bfloat16)
    active = normalize(hidden, gain_two, bias_two)
    return (values.astype(jnp.float32) + convolve(active, second)).astype(jnp.bfloat16)


def body(latents, conv_first, conv_second, gain_first, bias_first, gain_second, bias_second):
    segments = lax.axis_size("segment")
    micro = latents.shape[0]
    per_segment = micro // segments
    position = lax.axis_index("segment")
    small = jnp.stack([gain_first, bias_first, gain_second, bias_second], axis=1)
    small = lax.all_gather(small, "segment", axis=0, tiled=True)
    first = lax.all_gather(conv_first, "segment", axis=0, tiled=True)
    second = lax.all_gather(conv_second, "segment", axis=0, tiled=True)
    outs = []
    for index in range(per_segment):
        values = lax.dynamic_index_in_dim(
            latents, position * per_segment + index, 0, keepdims=False
        )
        for layer in range(first.shape[0]):
            gains = small[layer]
            values = residual_block(
                values, (first[layer], second[layer], gains[0], gains[1], gains[2], gains[3])
            )
        outs.append(values)
    return jnp.stack(outs)


def solution(mesh):
    in_specs = (
        P(None, "tm", "rows", None, None),
        P("segment", None, None, None, None, None),
        P("segment", None, None, None, None, None),
        P("segment", None),
        P("segment", None),
        P("segment", None),
        P("segment", None),
    )
    out_specs = P("segment", "tm", "rows", None, None)
    return jax.shard_map(body, mesh=mesh, in_specs=in_specs, out_specs=out_specs, check_vma=False)
```

profile of v0, /device:TPU:1, one launch (start us, length us, event | category | flops | bytes accessed | tf_op | source)
XLA Modules:
  0.0 295.1 jit_solution(6094731690513591556)
XLA Ops:
  8.6 10.8 %all-reduce.15 = (f32[32]{0:T(128)S(1)}, f32[32]{0:T(128)S(1)}) all-reduce(f32[32]{0:T(128)S(1)} %reduce_sum.195, f32[32]{0:T(128)S(1)} %reduce_sum.189), channel_id=1, replica_groups=mesh['rows'=4,'segment'=4,'tm'=2] {'rows'}, use_global_device_ids=true, to_apply=%region_5.6 | all-reduce | flops 64 | bytes 512 | tf_op jit(solution)/shard_map/psum | solution.py:35
  19.9 6.7 %all_gather.9 = bf16[4,4,128]{2,1,0:T(4,128)(2,1)S(1)} all-gather(bf16[1,4,128]{2,1,0:T(4,128)(2,1)S(1)} %pad_maximum_fusion.8), channel_id=1, replica_groups=mesh['rows'=4,'segment'=4,'tm'=2] {'segment'}, dimensions={0}, use_global_device_ids=true | all-gather | bytes 5120 | tf_op jit(solution)/shard_map/all_gather | solution.py:79
  28.1 4.9 %collective-permute-done = bf16[2,2,128,128]{3,2,1,0:T(8,128)(2,1)S(1)} collective-permute-done((bf16[2,2,128,128]{3,2,1,0:T(8,128)(2,1)S(1)}, bf16[2,2,128,128]{3,2,1,0:T(8,128)(2,1)S(1)}, u32[]{:S(2)}, u32[]{:S(2)}) %collective-permute-start) | collective-permute-done | bytes 131104 | tf_op jit(solution)/shard_map/ppermute | solution.py:15
  38.8 4.0 %collective-permute-done.2 = bf16[6,1,128,128]{3,2,1,0:T(8,128)(2,1)S(1)} collective-permute-done((bf16[6,1,128,128]{3,2,1,0:T(8,128)(2,1)S(1)}, bf16[6,1,128,128]{3,2,1,0:T(8,128)(2,1)S(1)}, u32[]{:S(2)}, u32[]{:S(2)}) %collective-permute-start.2) | collective-permute-done | bytes 196640 | tf_op jit(solution)/shard_map/ppermute | solution.py:26
  43.8 14.8 %all-gather.3.cloned.1.call-done = bf16[4,3,3,3,128,128]{5,4,3,2,1,0:T(8,128)(2,1)} async-done(((bf16[1,3,3,3,128,128]{5,4,3,2,1,0:T(8,128)(2,1)}), bf16[4,3,3,3,128,128]{5,4,3,2,1,0:T(8,128)(2,1)}) %all-gather.3.cloned.1.call-update) | async-done | bytes 3538960 | tf_op jit(solution)/shard_map/all_gather | solution.py:80
  62.4 9.7 %all-reduce.14 = (f32[32]{0:T(128)S(1)}, f32[32]{0:T(128)S(1)}) all-reduce(f32[32]{0:T(128)S(1)} %reduce_sum.204, f32[32]{0:T(128)S(1)} %reduce_sum.201), channel_id=1, replica_groups=mesh['rows'=4,'segment'=4,'tm'=2] {'rows'}, use_global_device_ids=true, to_apply=%region_11.12 | all-reduce | flops 64 | bytes 512 | tf_op jit(solution)/shard_map/psum | solution.py:35
  74.4 3.5 %collective-permute-done.3 = bf16[2,2,128,128]{3,2,1,0:T(8,128)(2,1)S(1)} collective-permute-done((bf16[2,2,128,128]{3,2,1,0:T(8,128)(2,1)S(1)}, bf16[2,2,128,128]{3,2,1,0:T(8,128)(2,1)S(1)}, u32[]{:S(2)}, u32[]{:S(2)}) %collective-permute-start.3) | collective-permute-done | bytes 131104 | tf_op jit(solution)/shard_map/ppermute | solution.py:15
  83.6 3.9 %collective-permute-done.5 = bf16[6,1,128,128]{3,2,1,0:T(8,128)(2,1)S(1)} collective-permute-done((bf16[6,1,128,128]{3,2,1,0:T(8,128)(2,1)S(1)}, bf16[6,1,128,128]{3,2,1,0:T(8,128)(2,1)S(1)}, u32[]{:S(2)}, u32[]{:S(2)}) %collective-permute-start.5) | collective-permute-done | bytes 196640 | tf_op jit(solution)/shard_map/ppermute | solution.py:26
  88.5 19.2 %all-gather.5.cloned.1.call-done = bf16[4,3,3,3,128,128]{5,4,3,2,1,0:T(8,128)(2,1)} async-done(((bf16[1,3,3,3,128,128]{5,4,3,2,1,0:T(8,128)(2,1)}), bf16[4,3,3,3,128,128]{5,4,3,2,1,0:T(8,128)(2,1)}) %all-gather.5.cloned.1.call-update) | async-done | bytes 3538960 | tf_op jit(solution)/shard_map/all_gather | solution.py:81
  112.0 9.7 %all-reduce.13 = (f32[32]{0:T(128)S(1)}, f32[32]{0:T(128)S(1)}) all-reduce(f32[32]{0:T(128)S(1)} %reduce_sum.216, f32[32]{0:T(128)S(1)} %reduce_sum.210), channel_id=1, replica_groups=mesh['rows'=4,'segment'=4,'tm'=2] {'rows'}, use_global_device_ids=true, to_apply=%region_17.18 | all-reduce | flops 64 | bytes 512 | tf_op jit(solution)/shard_map/psum | solution.py:35
  123.6 3.5 %collective-permute-done.6 = bf16[2,2,128,128]{3,2,1,0:T(8,128)(2,1)S(1)} collective-permute-done((bf16[2,2,128,128]{3,2,1,0:T(8,128)(2,1)S(1)}, bf16[2,2,128,128]{3,2,1,0:T(8,128)(2,1)S(1)}, u32[]{:S(2)}, u32[]{:S(2)}) %collective-permute-start.6) | collective-permute-done | bytes 131104 | tf_op jit(solution)/shard_map/ppermute | solution.py:15
  132.8 3.9 %collective-permute-done.8 = bf16[6,1,128,128]{3,2,1,0:T(8,128)(2,1)S(1)} collective-permute-done((bf16[6,1,128,128]{3,2,1,0:T(8,128)(2,1)S(1)}, bf16[6,1,128,128]{3,2,1,0:T(8,128)(2,1)S(1)}, u32[]{:S(2)}, u32[]{:S(2)}) %collective-permute-start.8) | collective-permute-done | bytes 196640 | tf_op jit(solution)/shard_map/ppermute | solution.py:26
  141.5 6.6 %all-reduce.12 = (f32[32]{0:T(128)S(1)}, f32[32]{0:T(128)S(1)}) all-reduce(f32[32]{0:T(128)S(1)} %reduce_sum.225, f32[32]{0:T(128)S(1)} %reduce_sum.219), channel_id=1, replica_groups=mesh['rows'=4,'segment'=4,'tm'=2] {'rows'}, use_global_device_ids=true, to_apply=%region_23.24 | all-reduce | flops 64 | bytes 512 | tf_op jit(solution)/shard_map/psum | solution.py:35
  150.5 4.1 %collective-permute-done.9 = bf16[2,2,128,128]{3,2,1,0:T(8,128)(2,1)S(1)} collective-permute-done((bf16[2,2,128,128]{3,2,1,0:T(8,128)(2,1)S(1)}, bf16[2,2,128,128]{3,2,1,0:T(8,128)(2,1)S(1)}, u32[]{:S(2)}, u32[]{:S(2)}) %collective-permute-start.9) | collective-permute-done | bytes 131104 | tf_op jit(solution)/shard_map/ppermute | solution.py:15
  161.8 3.8 %collective-permute-done.11 = bf16[6,1,128,128]{3,2,1,0:T(8,128)(2,1)S(1)} collective-permute-done((bf16[6,1,128,128]{3,2,1,0:T(8,128)(2,1)S(1)}, bf16[6,1,128,128]{3,2,1,0:T(8,128)(2,1)S(1)}, u32[]{:S(2)}, u32[]{:S(2)}) %collective-permute-start.11) | collective-permute-done | bytes 196640 | tf_op jit(solution)/shard_map/ppermute | solution.py:26
  170.9 7.0 %all-reduce.11 = (f32[32]{0:T(128)S(1)}, f32[32]{0:T(128)S(1)}) all-reduce(f32[32]{0:T(128)S(1)} %reduce_sum.234, f32[32]{0:T(128)S(1)} %reduce_sum.231), channel_id=1, replica_groups=mesh['rows'=4,'segment'=4,'tm'=2] {'rows'}, use_global_device_ids=true, to_apply=%region_29.30 | all-reduce | flops 64 | bytes 512 | tf_op jit(solution)/shard_map/psum | solution.py:35
  179.8 3.8 %collective-permute-done.12 = bf16[2,2,128,128]{3,2,1,0:T(8,128)(2,1)S(1)} collective-permute-done((bf16[2,2,128,128]{3,2,1,0:T(8,128)(2,1)S(1)}, bf16[2,2,128,128]{3,2,1,0:T(8,128)(2,1)S(1)}, u32[]{:S(2)}, u32[]{:S(2)}) %collective-permute-start.12) | collective-permute-done | bytes 131104 | tf_op jit(solution)/shard_map/ppermute | solution.py:15
  183.6 3.3 %collective-permute-start.13 = (bf16[6,1,128,128]{3,2,1,0:T(8,128)(2,1)S(1)}, bf16[6,1,128,128]{3,2,1,0:T(8,128)(2,1)S(1)}, u32[]{:S(2)}, u32[]{:S(2)}) collective-permute-start(bf16[6,1,128,128]{3,2,1,0:T(8,128)(2,1)S(1)} %get-tuple-element.48), channel_id=1, source_target_pairs={{0,8},{8,16},{16,24},{1,9},{9,17},{17,25},{2,10},{10,18},{18,26},{... | collective-permute-start | bytes 589832 | tf_op jit(solution)/shard_map/ppermute | solution.py:23
  191.1 3.8 %collective-permute-done.14 = bf16[6,1,128,128]{3,2,1,0:T(8,128)(2,1)S(1)} collective-permute-done((bf16[6,1,128,128]{3,2,1,0:T(8,128)(2,1)S(1)}, bf16[6,1,128,128]{3,2,1,0:T(8,128)(2,1)S(1)}, u32[]{:S(2)}, u32[]{:S(2)}) %collective-permute-start.14) | collective-permute-done | bytes 196640 | tf_op jit(solution)/shard_map/ppermute | solution.py:26
  199.7 7.2 %all-reduce.10 = (f32[32]{0:T(128)S(1)}, f32[32]{0:T(128)S(1)}) all-reduce(f32[32]{0:T(128)S(1)} %reduce_sum.291, f32[32]{0:T(128)S(1)} %reduce_sum.288), channel_id=1, replica_groups=mesh['rows'=4,'segment'=4,'tm'=2] {'rows'}, use_global_device_ids=true, to_apply=%region_35.36 | all-reduce | flops 64 | bytes 512 | tf_op jit(solution)/shard_map/psum | solution.py:35
  209.2 3.8 %collective-permute-done.15 = bf16[2,2,128,128]{3,2,1,0:T(8,128)(2,1)S(1)} collective-permute-done((bf16[2,2,128,128]{3,2,1,0:T(8,128)(2,1)S(1)}, bf16[2,2,128,128]{3,2,1,0:T(8,128)(2,1)S(1)}, u32[]{:S(2)}, u32[]{:S(2)}) %collective-permute-start.15) | collective-permute-done | bytes 131104 | tf_op jit(solution)/shard_map/ppermute | solution.py:15
  213.0 3.3 %collective-permute-start.16 = (bf16[6,1,128,128]{3,2,1,0:T(8,128)(2,1)S(1)}, bf16[6,1,128,128]{3,2,1,0:T(8,128)(2,1)S(1)}, u32[]{:S(2)}, u32[]{:S(2)}) collective-permute-start(bf16[6,1,128,128]{3,2,1,0:T(8,128)(2,1)S(1)} %get-tuple-element.46), channel_id=1, source_target_pairs={{0,8},{8,16},{16,24},{1,9},{9,17},{17,25},{2,10},{10,18},{18,26},{... | collective-permute-start | bytes 589832 | tf_op jit(solution)/shard_map/ppermute | solution.py:23
  220.5 3.8 %collective-permute-done.17 = bf16[6,1,128,128]{3,2,1,0:T(8,128)(2,1)S(1)} collective-permute-done((bf16[6,1,128,128]{3,2,1,0:T(8,128)(2,1)S(1)}, bf16[6,1,128,128]{3,2,1,0:T(8,128)(2,1)S(1)}, u32[]{:S(2)}, u32[]{:S(2)}) %collective-permute-start.17) | collective-permute-done | bytes 196640 | tf_op jit(solution)/shard_map/ppermute | solution.py:26
  229.6 7.0 %all-reduce.9 = (f32[32]{0:T(128)S(1)}, f32[32]{0:T(128)S(1)}) all-reduce(f32[32]{0:T(128)S(1)} %reduce_sum.297, f32[32]{0:T(128)S(1)} %reduce_sum.294), channel_id=1, replica_groups=mesh['rows'=4,'segment'=4,'tm'=2] {'rows'}, use_global_device_ids=true, to_apply=%region_41.42 | all-reduce | flops 64 | bytes 512 | tf_op jit(solution)/shard_map/psum | solution.py:35
  238.5 3.8 %collective-permute-done.18 = bf16[2,2,128,128]{3,2,1,0:T(8,128)(2,1)S(1)} collective-permute-done((bf16[2,2,128,128]{3,2,1,0:T(8,128)(2,1)S(1)}, bf16[2,2,128,128]{3,2,1,0:T(8,128)(2,1)S(1)}, u32[]{:S(2)}, u32[]{:S(2)}) %collective-permute-start.18) | collective-permute-done | bytes 131104 | tf_op jit(solution)/shard_map/ppermute | solution.py:15
  242.4 3.3 %collective-permute-start.19 = (bf16[6,1,128,128]{3,2,1,0:T(8,128)(2,1)S(1)}, bf16[6,1,128,128]{3,2,1,0:T(8,128)(2,1)S(1)}, u32[]{:S(2)}, u32[]{:S(2)}) collective-permute-start(bf16[6,1,128,128]{3,2,1,0:T(8,128)(2,1)S(1)} %get-tuple-element.44), channel_id=1, source_target_pairs={{0,8},{8,16},{16,24},{1,9},{9,17},{17,25},{2,10},{10,18},{18,26},{... | collective-permute-start | bytes 589832 | tf_op jit(solution)/shard_map/ppermute | solution.py:23
  249.8 3.8 %collective-permute-done.20 = bf16[6,1,128,128]{3,2,1,0:T(8,128)(2,1)S(1)} collective-permute-done((bf16[6,1,128,128]{3,2,1,0:T(8,128)(2,1)S(1)}, bf16[6,1,128,128]{3,2,1,0:T(8,128)(2,1)S(1)}, u32[]{:S(2)}, u32[]{:S(2)}) %collective-permute-start.20) | collective-permute-done | bytes 196640 | tf_op jit(solution)/shard_map/ppermute | solution.py:26
  254.7 3.3 %fusion.90 = (f32[128]{0:T(128)S(1)}, f32[128]{0:T(128)S(1)}, bf16[4,2,8,17,128]{4,2,3,1,0:T(8,128)(2,1)S(1)}) fusion(pred[8,17]{0,1:T(8,128)(4,1)S(1)} %copy-done.5, bf16[4,3,3,3,128,128]{5,4,3,2,1,0:T(8,128)(2,1)} %all-gather.3.cloned.1.call-done, bf16[6,4,1,7,2,128]{5,3,4,1,0,2:T(8,128)(2,1)S(1)} %slice.297, bf16[6,4,1,8,17,128]{5,3,4,1,0,2:T(8,128)(2,1)S(1)} %copy.92), kind=kOutput, calls=%fused_computation.146 | convolution fusion | flops 966508288 | bytes 2086024 | tf_op jit(solution)/shard_map/conv_general_dilated | solution.py:54
  258.5 7.0 %all-reduce.8 = (f32[32]{0:T(128)S(1)}, f32[32]{0:T(128)S(1)}) all-reduce(f32[32]{0:T(128)S(1)} %reduce_sum.303, f32[32]{0:T(128)S(1)} %reduce_sum.300), channel_id=1, replica_groups=mesh['rows'=4,'segment'=4,'tm'=2] {'rows'}, use_global_device_ids=true, to_apply=%region_47.48 | all-reduce | flops 64 | bytes 512 | tf_op jit(solution)/shard_map/psum | solution.py:35
  267.7 3.8 %collective-permute-done.21 = bf16[2,2,128,128]{3,2,1,0:T(8,128)(2,1)S(1)} collective-permute-done((bf16[2,2,128,128]{3,2,1,0:T(8,128)(2,1)S(1)}, bf16[2,2,128,128]{3,2,1,0:T(8,128)(2,1)S(1)}, u32[]{:S(2)}, u32[]{:S(2)}) %collective-permute-start.21) | collective-permute-done | bytes 131104 | tf_op jit(solution)/shard_map/ppermute | solution.py:15
  271.6 3.3 %collective-permute-start.22 = (bf16[6,1,128,128]{3,2,1,0:T(8,128)(2,1)S(1)}, bf16[6,1,128,128]{3,2,1,0:T(8,128)(2,1)S(1)}, u32[]{:S(2)}, u32[]{:S(2)}) collective-permute-start(bf16[6,1,128,128]{3,2,1,0:T(8,128)(2,1)S(1)} %get-tuple-element.42), channel_id=1, source_target_pairs={{0,8},{8,16},{16,24},{1,9},{9,17},{17,25},{2,10},{10,18},{18,26},{... | collective-permute-start | bytes 589832 | tf_op jit(solution)/shard_map/ppermute | solution.py:23
  279.0 3.8 %collective-permute-done.23 = bf16[6,1,128,128]{3,2,1,0:T(8,128)(2,1)S(1)} collective-permute-done((bf16[6,1,128,128]{3,2,1,0:T(8,128)(2,1)S(1)}, bf16[6,1,128,128]{3,2,1,0:T(8,128)(2,1)S(1)}, u32[]{:S(2)}, u32[]{:S(2)}) %collective-permute-start.23) | collective-permute-done | bytes 196640 | tf_op jit(solution)/shard_map/ppermute | solution.py:26
  (210 shorter events, 96.5 us)
Async XLA Ops:
  6.5 1.5 copy-start
  6.5 13.3 %copy-start.1 = (bf16[1,128]{1,0:T(2,128)(2,1)S(1)}, bf16[1,128]{1,0:T(2,128)(2,1)}, u32[]{:S(2)}) copy-start(bf16[1,128]{1,0:T(2,128)(2,1)} %param.13) | copy-start | bytes 772
  6.5 13.3 %copy-start.2 = (bf16[1,128]{1,0:T(2,128)(2,1)S(1)}, bf16[1,128]{1,0:T(2,128)(2,1)}, u32[]{:S(2)}) copy-start(bf16[1,128]{1,0:T(2,128)(2,1)} %param.12) | copy-start | bytes 772
  6.5 13.3 %copy-start.3 = (bf16[1,128]{1,0:T(2,128)(2,1)S(1)}, bf16[1,128]{1,0:T(2,128)(2,1)}, u32[]{:S(2)}) copy-start(bf16[1,128]{1,0:T(2,128)(2,1)} %param.11) | copy-start | bytes 772
  6.5 13.3 %copy-start.4 = (bf16[1,128]{1,0:T(2,128)(2,1)S(1)}, bf16[1,128]{1,0:T(2,128)(2,1)}, u32[]{:S(2)}) copy-start(bf16[1,128]{1,0:T(2,128)(2,1)} %param.10) | copy-start | bytes 772
  6.5 52.1 %all-gather.3.cloned.1.call-start = ((), (), s32[]{:S(2)}) async-start(), calls=%async_computation | async-start | bytes 4423680 | tf_op jit(solution)/shard_map/all_gather | solution.py:80
  7.3 100.5 %all-gather.5.cloned.1.call-start = ((), (), s32[]{:S(2)}) async-start(), calls=%async_computation.1 | async-start | bytes 4423680 | tf_op jit(solution)/shard_map/all_gather | solution.py:81
  26.8 6.2 %collective-permute-start = (bf16[2,2,128,128]{3,2,1,0:T(8,128)(2,1)S(1)}, bf16[2,2,128,128]{3,2,1,0:T(8,128)(2,1)S(1)}, u32[]{:S(2)}, u32[]{:S(2)}) collective-permute-start(bf16[2,2,128,128]{3,2,1,0:T(8,128)(2,1)S(1)} %slice.246), channel_id=1, source_target_pairs={{0,1},{2,3},{4,5},{6,7},{8,9},{10,11},{12,13},{14,15},{16,17},{18,... | collective-permute-start | bytes 393224 | tf_op jit(solution)/shard_map/ppermute | solution.py:15
  33.1 5.7 %collective-permute-start.1 = (bf16[6,1,128,128]{3,2,1,0:T(8,128)(2,1)S(1)}, bf16[6,1,128,128]{3,2,1,0:T(8,128)(2,1)S(1)}, u32[]{:S(2)}, u32[]{:S(2)}) collective-permute-start(bf16[6,1,128,128]{3,2,1,0:T(8,128)(2,1)S(1)} %get-tuple-element.56), channel_id=1, source_target_pairs={{0,8},{8,16},{16,24},{1,9},{9,17},{17,25},{2,10},{10,18},{18,26},{... | collective-permute-start | bytes 589832 | tf_op jit(solution)/shard_map/ppermute | solution.py:23
  34.4 8.4 %collective-permute-start.2 = (bf16[6,1,128,128]{3,2,1,0:T(8,128)(2,1)S(1)}, bf16[6,1,128,128]{3,2,1,0:T(8,128)(2,1)S(1)}, u32[]{:S(2)}, u32[]{:S(2)}) collective-permute-start(bf16[6,1,128,128]{3,2,1,0:T(8,128)(2,1)S(1)} %get-tuple-element.57), channel_id=1, source_target_pairs={{8,0},{16,8},{24,16},{9,1},{17,9},{25,17},{10,2},{18,10},{26,18},{... | collective-permute-start | bytes 589832 | tf_op jit(solution)/shard_map/ppermute | solution.py:26
  43.3 15.3 %copy-start.5 = (pred[8,17]{0,1:T(8,128)(4,1)S(1)}, pred[8,17]{0,1:T(8,128)(4,1)}, u32[]{:S(2)}) copy-start(pred[8,17]{0,1:T(8,128)(4,1)} %constant.110) | copy-start | bytes 412
  73.1 4.8 %collective-permute-start.3 = (bf16[2,2,128,128]{3,2,1,0:T(8,128)(2,1)S(1)}, bf16[2,2,128,128]{3,2,1,0:T(8,128)(2,1)S(1)}, u32[]{:S(2)}, u32[]{:S(2)}) collective-permute-start(bf16[2,2,128,128]{3,2,1,0:T(8,128)(2,1)S(1)} %slice.254), channel_id=1, source_target_pairs={{0,1},{2,3},{4,5},{6,7},{8,9},{10,11},{12,13},{14,15},{16,17},{18,... | collective-permute-start | bytes 393224 | tf_op jit(solution)/shard_map/ppermute | solution.py:15
  77.9 5.7 %collective-permute-start.4 = (bf16[6,1,128,128]{3,2,1,0:T(8,128)(2,1)S(1)}, bf16[6,1,128,128]{3,2,1,0:T(8,128)(2,1)S(1)}, u32[]{:S(2)}, u32[]{:S(2)}) collective-permute-start(bf16[6,1,128,128]{3,2,1,0:T(8,128)(2,1)S(1)} %get-tuple-element.54), channel_id=1, source_target_pairs={{0,8},{8,16},{16,24},{1,9},{9,17},{17,25},{2,10},{10,18},{18,26},{... | collective-permute-start | bytes 589832 | tf_op jit(solution)/shard_map/ppermute | solution.py:23
  79.2 8.2 %collective-permute-start.5 = (bf16[6,1,128,128]{3,2,1,0:T(8,128)(2,1)S(1)}, bf16[6,1,128,128]{3,2,1,0:T(8,128)(2,1)S(1)}, u32[]{:S(2)}, u32[]{:S(2)}) collective-permute-start(bf16[6,1,128,128]{3,2,1,0:T(8,128)(2,1)S(1)} %get-tuple-element.55), channel_id=1, source_target_pairs={{8,0},{16,8},{24,16},{9,1},{17,9},{25,17},{10,2},{18,10},{26,18},{... | collective-permute-start | bytes 589832 | tf_op jit(solution)/shard_map/ppermute | solution.py:26
  122.3 4.8 %collective-permute-start.6 = (bf16[2,2,128,128]{3,2,1,0:T(8,128)(2,1)S(1)}, bf16[2,2,128,128]{3,2,1,0:T(8,128)(2,1)S(1)}, u32[]{:S(2)}, u32[]{:S(2)}) collective-permute-start(bf16[2,2,128,128]{3,2,1,0:T(8,128)(2,1)S(1)} %slice.262), channel_id=1, source_target_pairs={{0,1},{2,3},{4,5},{6,7},{8,9},{10,11},{12,13},{14,15},{16,17},{18,... | collective-permute-start | bytes 393224 | tf_op jit(solution)/shard_map/ppermute | solution.py:15
  127.2 5.7 %collective-permute-start.7 = (bf16[6,1,128,128]{3,2,1,0:T(8,128)(2,1)S(1)}, bf16[6,1,128,128]{3,2,1,0:T(8,128)(2,1)S(1)}, u32[]{:S(2)}, u32[]{:S(2)}) collective-permute-start(bf16[6,1,128,128]{3,2,1,0:T(8,128)(2,1)S(1)} %get-tuple-element.52), channel_id=1, source_target_pairs={{0,8},{8,16},{16,24},{1,9},{9,17},{17,25},{2,10},{10,18},{18,26},{... | collective-permute-start | bytes 589832 | tf_op jit(solution)/shard_map/ppermute | solution.py:23
  128.5 8.2 %collective-permute-start.8 = (bf16[6,1,128,128]{3,2,1,0:T(8,128)(2,1)S(1)}, bf16[6,1,128,128]{3,2,1,0:T(8,128)(2,1)S(1)}, u32[]{:S(2)}, u32[]{:S(2)}) collective-permute-start(bf16[6,1,128,128]{3,2,1,0:T(8,128)(2,1)S(1)} %get-tuple-element.53), channel_id=1, source_target_pairs={{8,0},{16,8},{24,16},{9,1},{17,9},{25,17},{10,2},{18,10},{26,18},{... | collective-permute-start | bytes 589832 | tf_op jit(solution)/shard_map/ppermute | solution.py:26
  149.2 5.4 %collective-permute-start.9 = (bf16[2,2,128,128]{3,2,1,0:T(8,128)(2,1)S(1)}, bf16[2,2,128,128]{3,2,1,0:T(8,128)(2,1)S(1)}, u32[]{:S(2)}, u32[]{:S(2)}) collective-permute-start(bf16[2,2,128,128]{3,2,1,0:T(8,128)(2,1)S(1)} %slice.270), channel_id=1, source_target_pairs={{0,1},{2,3},{4,5},{6,7},{8,9},{10,11},{12,13},{14,15},{16,17},{18,... | collective-permute-start | bytes 393224 | tf_op jit(solution)/shard_map/ppermute | solution.py:15
  154.6 7.2 %collective-permute-start.10 = (bf16[6,1,128,128]{3,2,1,0:T(8,128)(2,1)S(1)}, bf16[6,1,128,128]{3,2,1,0:T(8,128)(2,1)S(1)}, u32[]{:S(2)}, u32[]{:S(2)}) collective-permute-start(bf16[6,1,128,128]{3,2,1,0:T(8,128)(2,1)S(1)} %get-tuple-element.50), channel_id=1, source_target_pairs={{0,8},{8,16},{16,24},{1,9},{9,17},{17,25},{2,10},{10,18},{18,26},{... | collective-permute-start | bytes 589832 | tf_op jit(solution)/shard_map/ppermute | solution.py:23
  157.7 7.9 %collective-permute-start.11 = (bf16[6,1,128,128]{3,2,1,0:T(8,128)(2,1)S(1)}, bf16[6,1,128,128]{3,2,1,0:T(8,128)(2,1)S(1)}, u32[]{:S(2)}, u32[]{:S(2)}) collective-permute-start(bf16[6,1,128,128]{3,2,1,0:T(8,128)(2,1)S(1)} %get-tuple-element.51), channel_id=1, source_target_pairs={{8,0},{16,8},{24,16},{9,1},{17,9},{25,17},{10,2},{18,10},{26,18},{... | collective-permute-start | bytes 589832 | tf_op jit(solution)/shard_map/ppermute | solution.py:26
  178.5 5.1 %collective-permute-start.12 = (bf16[2,2,128,128]{3,2,1,0:T(8,128)(2,1)S(1)}, bf16[2,2,128,128]{3,2,1,0:T(8,128)(2,1)S(1)}, u32[]{:S(2)}, u32[]{:S(2)}) collective-permute-start(bf16[2,2,128,128]{3,2,1,0:T(8,128)(2,1)S(1)} %slice.278), channel_id=1, source_target_pairs={{0,1},{2,3},{4,5},{6,7},{8,9},{10,11},{12,13},{14,15},{16,17},{18,... | collective-permute-start | bytes 393224 | tf_op jit(solution)/shard_map/ppermute | solution.py:15
  183.6 7.5 %collective-permute-start.13 = (bf16[6,1,128,128]{3,2,1,0:T(8,128)(2,1)S(1)}, bf16[6,1,128,128]{3,2,1,0:T(8,128)(2,1)S(1)}, u32[]{:S(2)}, u32[]{:S(2)}) collective-permute-start(bf16[6,1,128,128]{3,2,1,0:T(8,128)(2,1)S(1)} %get-tuple-element.48), channel_id=1, source_target_pairs={{0,8},{8,16},{16,24},{1,9},{9,17},{17,25},{2,10},{10,18},{18,26},{... | collective-permute-start | bytes 589832 | tf_op jit(solution)/shard_map/ppermute | solution.py:23
  187.0 7.9 %collective-permute-start.14 = (bf16[6,1,128,128]{3,2,1,0:T(8,128)(2,1)S(1)}, bf16[6,1,128,128]{3,2,1,0:T(8,128)(2,1)S(1)}, u32[]{:S(2)}, u32[]{:S(2)}) collective-permute-start(bf16[6,1,128,128]{3,2,1,0:T(8,128)(2,1)S(1)} %get-tuple-element.49), channel_id=1, source_target_pairs={{8,0},{16,8},{24,16},{9,1},{17,9},{25,17},{10,2},{18,10},{26,18},{... | collective-permute-start | bytes 589832 | tf_op jit(solution)/shard_map/ppermute | solution.py:26
  207.9 5.1 %collective-permute-start.15 = (bf16[2,2,128,128]{3,2,1,0:T(8,128)(2,1)S(1)}, bf16[2,2,128,128]{3,2,1,0:T(8,128)(2,1)S(1)}, u32[]{:S(2)}, u32[]{:S(2)}) collective-permute-start(bf16[2,2,128,128]{3,2,1,0:T(8,128)(2,1)S(1)} %slice.286), channel_id=1, source_target_pairs={{0,1},{2,3},{4,5},{6,7},{8,9},{10,11},{12,13},{14,15},{16,17},{18,... | collective-permute-start | bytes 393224 | tf_op jit(solution)/shard_map/ppermute | solution.py:15
  213.0 7.5 %collective-permute-start.16 = (bf16[6,1,128,128]{3,2,1,0:T(8,128)(2,1)S(1)}, bf16[6,1,128,128]{3,2,1,0:T(8,128)(2,1)S(1)}, u32[]{:S(2)}, u32[]{:S(2)}) collective-permute-start(bf16[6,1,128,128]{3,2,1,0:T(8,128)(2,1)S(1)} %get-tuple-element.46), channel_id=1, source_target_pairs={{0,8},{8,16},{16,24},{1,9},{9,17},{17,25},{2,10},{10,18},{18,26},{... | collective-permute-start | bytes 589832 | tf_op jit(solution)/shard_map/ppermute | solution.py:23
  216.4 7.9 %collective-permute-start.17 = (bf16[6,1,128,128]{3,2,1,0:T(8,128)(2,1)S(1)}, bf16[6,1,128,128]{3,2,1,0:T(8,128)(2,1)S(1)}, u32[]{:S(2)}, u32[]{:S(2)}) collective-permute-start(bf16[6,1,128,128]{3,2,1,0:T(8,128)(2,1)S(1)} %get-tuple-element.47), channel_id=1, source_target_pairs={{8,0},{16,8},{24,16},{9,1},{17,9},{25,17},{10,2},{18,10},{26,18},{... | collective-permute-start | bytes 589832 | tf_op jit(solution)/shard_map/ppermute | solution.py:26
  237.2 5.1 %collective-permute-start.18 = (bf16[2,2,128,128]{3,2,1,0:T(8,128)(2,1)S(1)}, bf16[2,2,128,128]{3,2,1,0:T(8,128)(2,1)S(1)}, u32[]{:S(2)}, u32[]{:S(2)}) collective-permute-start(bf16[2,2,128,128]{3,2,1,0:T(8,128)(2,1)S(1)} %slice.294), channel_id=1, source_target_pairs={{0,1},{2,3},{4,5},{6,7},{8,9},{10,11},{12,13},{14,15},{16,17},{18,... | collective-permute-start | bytes 393224 | tf_op jit(solution)/shard_map/ppermute | solution.py:15
  242.4 7.5 %collective-permute-start.19 = (bf16[6,1,128,128]{3,2,1,0:T(8,128)(2,1)S(1)}, bf16[6,1,128,128]{3,2,1,0:T(8,128)(2,1)S(1)}, u32[]{:S(2)}, u32[]{:S(2)}) collective-permute-start(bf16[6,1,128,128]{3,2,1,0:T(8,128)(2,1)S(1)} %get-tuple-element.44), channel_id=1, source_target_pairs={{0,8},{8,16},{16,24},{1,9},{9,17},{17,25},{2,10},{10,18},{18,26},{... | collective-permute-start | bytes 589832 | tf_op jit(solution)/shard_map/ppermute | solution.py:23
  245.7 7.9 %collective-permute-start.20 = (bf16[6,1,128,128]{3,2,1,0:T(8,128)(2,1)S(1)}, bf16[6,1,128,128]{3,2,1,0:T(8,128)(2,1)S(1)}, u32[]{:S(2)}, u32[]{:S(2)}) collective-permute-start(bf16[6,1,128,128]{3,2,1,0:T(8,128)(2,1)S(1)} %get-tuple-element.45), channel_id=1, source_target_pairs={{8,0},{16,8},{24,16},{9,1},{17,9},{25,17},{10,2},{18,10},{26,18},{... | collective-permute-start | bytes 589832 | tf_op jit(solution)/shard_map/ppermute | solution.py:26
  266.4 5.1 %collective-permute-start.21 = (bf16[2,2,128,128]{3,2,1,0:T(8,128)(2,1)S(1)}, bf16[2,2,128,128]{3,2,1,0:T(8,128)(2,1)S(1)}, u32[]{:S(2)}, u32[]{:S(2)}) collective-permute-start(bf16[2,2,128,128]{3,2,1,0:T(8,128)(2,1)S(1)} %slice.302), channel_id=1, source_target_pairs={{0,1},{2,3},{4,5},{6,7},{8,9},{10,11},{12,13},{14,15},{16,17},{18,... | collective-permute-start | bytes 393224 | tf_op jit(solution)/shard_map/ppermute | solution.py:15
  271.6 7.5 %collective-permute-start.22 = (bf16[6,1,128,128]{3,2,1,0:T(8,128)(2,1)S(1)}, bf16[6,1,128,128]{3,2,1,0:T(8,128)(2,1)S(1)}, u32[]{:S(2)}, u32[]{:S(2)}) collective-permute-start(bf16[6,1,128,128]{3,2,1,0:T(8,128)(2,1)S(1)} %get-tuple-element.42), channel_id=1, source_target_pairs={{0,8},{8,16},{16,24},{1,9},{9,17},{17,25},{2,10},{10,18},{18,26},{... | collective-permute-start | bytes 589832 | tf_op jit(solution)/shard_map/ppermute | solution.py:23
  274.9 7.9 %collective-permute-start.23 = (bf16[6,1,128,128]{3,2,1,0:T(8,128)(2,1)S(1)}, bf16[6,1,128,128]{3,2,1,0:T(8,128)(2,1)S(1)}, u32[]{:S(2)}, u32[]{:S(2)}) collective-permute-start(bf16[6,1,128,128]{3,2,1,0:T(8,128)(2,1)S(1)} %get-tuple-element.43), channel_id=1, source_target_pairs={{8,0},{16,8},{24,16},{9,1},{17,9},{25,17},{10,2},{18,10},{26,18},{... | collective-permute-start | bytes 589832 | tf_op jit(solution)/shard_map/ppermute | solution.py:26
Sparse Core Ops, SparseCore 0:
  9.2 49.3 all-gather.2
  60.5 47.2 all-gather.4
where the time goes:
time: 297 us; the launch traced here: 295 us
  waiting for transfers between devices  120 us (40%)
  blocking collectives  71.5 us (24%)
  starting transfers between devices  41.5 us (14%)
  matrix products  26.5 us (9%)
  between operations  14.5 us (5%)
  local copies, waits for them, and re-layouts  13.6 us (5%)
  other arithmetic  7.41 us (2%)
    psum x8, blocking collectives, normalize(): lax.psum((jnp.sum(grouped, axis=(0, 1, 2, 4)), jnp.sum(grouped * grouped,...  64.8 us
    ppermute x8, waiting for transfers between devices, passed_along(): lax.ppermute(value, axis, [(source, source + steps) for source in range(i...  31.2 us
    ppermute x8, waiting for transfers between devices, padded_2(): lax.ppermute(lax.slice_in_dim(block, 0, width, axis=dim), axis, backward)  30.8 us
    conv_general_dilated x8, matrix products, convolve(): lax.conv_general_dilated(padded[None], kernel, (1, 1, 1), 'VALID', dimens...  26.5 us
    ppermute x8, waiting for transfers between devices, padded_2(): lax.ppermute(lax.slice_in_dim(block, block.shape[dim] - width, None, axis...  22.9 us
    ppermute x8, starting transfers between devices, padded_2(): lax.ppermute(lax.slice_in_dim(block, block.shape[dim] - width, None, axis...  20.3 us
    all_gather x1, waiting for transfers between devices, body(): second = lax.all_gather(conv_second, 'segment', axis=0, tiled=True)  19.2 us
    all_gather x1, waiting for transfers between devices, body(): first = lax.all_gather(conv_first, 'segment', axis=0, tiled=True)  14.8 us
  transfers between devices with their start and end apart: 26, of which 26 were waited for; matrix products, arithmetic and copies ran while one was open for 3% of the time, Pallas kernels for 0%

commit v1 on v0

--- a/solution.py
+++ b/solution.py
@@ -1,6 +1,10 @@
+import functools
+
 import jax
 import jax.numpy as jnp
 from jax import lax
+from jax.experimental import pallas as pl
+from jax.experimental.pallas import tpu as pltpu
 from jax.sharding import PartitionSpec as P
 
 GROUPS = 32
@@ -93,6 +97,451 @@
     return jnp.stack(outs)
 
 
+MESH = pl.DeviceIdType.MESH
+TILE = 16
+PIECES = 2
+
+
+def fused(
+    latents, first, second, small, out,
+    wbuf, gbuf, vin, values, raw, padded, act, edge_out, edge_in, stat_out, stat_in,
+    in_send, in_recv, own_sem, w_send, w_recv, w_own, g_send, g_recv,
+    e_send, e_recv, s_send, s_recv, o_send, o_recv,
+):
+    rows_count = lax.axis_size("rows")
+    cores = lax.axis_size("tm")
+    group = rows_count * cores
+    segments = lax.axis_size("segment")
+    z = lax.axis_index("rows")
+    core = lax.axis_index("tm")
+    seg = lax.axis_index("segment")
+    me = z * cores + core
+    _, frames_here, rows_here, _, channels = latents.shape
+    frames = frames_here * cores
+    height = rows_here * rows_count
+    lines = frames * height
+    taps = first.shape[0]
+    half = taps // 2
+    piece = half // PIECES
+    span_size = frames_here * height * TILE
+    convs = 2 * segments
+    across = seg + 1 - 2 * lax.rem(seg, 2)
+    along = lax.rem(seg + 2, 4)
+
+    def member(c):
+        return {"rows": c // cores, "tm": lax.rem(c, cores)}
+
+    partners = [lax.rem(me + d, group) for d in range(1, group)]
+    others = [lax.rem(seg + d, segments) for d in range(1, segments)]
+
+    barrier = pltpu.get_barrier_semaphore()
+    for c in partners:
+        pl.semaphore_signal(barrier, inc=1, device_id=member(c), device_id_type=MESH)
+    for s in others:
+        pl.semaphore_signal(barrier, inc=1, device_id={"segment": s}, device_id_type=MESH)
+    pl.semaphore_wait(barrier, group - 1 + segments - 1)
+
+    def start_owner(i, source):
+        k = 2 * seg + i
+        for q in range(PIECES):
+            rows = pl.ds(core * half + q * piece, piece)
+            for slot, target in enumerate((across, along)):
+                pltpu.make_async_remote_copy(
+                    source.at[rows], wbuf.at[k, rows],
+                    w_send.at[k, q, slot], w_recv.at[k, core, q],
+                    device_id={"segment": target}, device_id_type=MESH,
+                ).start()
+
+    start_owner(0, first)
+
+    def input_copy(c, sender):
+        dst = vin.at[
+            pl.ds(lax.rem(sender, cores) * frames_here, frames_here),
+            pl.ds((sender // cores) * rows_here, rows_here),
+        ]
+        src = latents.at[seg, :, :, pl.ds(c * TILE, TILE)]
+        return src, dst
+
+    for c in partners:
+        src, dst = input_copy(c, me)
+        pltpu.make_async_remote_copy(
+            src, dst, in_send.at[c], in_recv.at[me], device_id=member(c), device_id_type=MESH
+        ).start()
+    src, dst = input_copy(me, me)
+    own = pltpu.make_async_copy(src, dst, own_sem)
+    own.start()
+
+    for s in others:
+        pltpu.make_async_remote_copy(
+            small, gbuf.at[seg], g_send.at[s], g_recv.at[seg],
+            device_id={"segment": s}, device_id_type=MESH,
+        ).start()
+    gbuf[seg] = small[...]
+
+    for i, source in enumerate((first, second)):
+        pltpu.make_async_copy(source, wbuf.at[2 * seg + i], w_own.at[i]).start()
+    start_owner(1, second)
+
+    act[...] = jnp.zeros_like(act)
+    padded[...] = jnp.zeros_like(padded)
+
+    def relation(k):
+        block = k // 2
+        low = lax.rem(lax.rem(seg, 2) + lax.rem(block, 2), 2)
+        high = lax.rem(seg // 2 + block // 2, 2)
+        return low + 2 * high
+
+    def landed(k, part, q):
+        rows = pl.ds(part * half + q * piece, piece)
+        return pltpu.make_async_remote_copy(
+            wbuf.at[k, rows], wbuf.at[k, rows], w_send.at[k, q, 2], w_recv.at[k, part, q],
+            device_id={"tm": 1 - core}, device_id_type=MESH,
+        )
+
+    def forwarded(k, q):
+        rows = pl.ds(core * half + q * piece, piece)
+        target = jnp.where(core == 0, along, across)
+        return pltpu.make_async_remote_copy(
+            wbuf.at[k, rows], wbuf.at[k, rows], w_send.at[k, q, 0], w_recv.at[k, core, q],
+            device_id={"segment": target}, device_id_type=MESH,
+        )
+
+    def pump(k):
+        kind = relation(k)
+        for q in range(PIECES):
+
+            @pl.when(kind != 0)
+            def _():
+                landed(k, core, q).wait_recv()
+
+                @pl.when(kind == core + 1)
+                def _():
+                    forwarded(k, q).start()
+
+                landed(k, core, q).start()
+
+    def arrive(k):
+        kind = relation(k)
+
+        @pl.when(kind != 0)
+        def _():
+            for q in range(PIECES):
+                landed(k, 1 - core, q).wait_recv()
+
+        @pl.when(kind == 0)
+        def _():
+            i = lax.rem(k, 2)
+            pltpu.make_async_copy(first, wbuf.at[k], w_own.at[i]).wait()
+
+    def put(k, span, fresh):
+        raw[pl.ds(span * span_size, span_size)] = fresh
+        total = jnp.sum(fresh, axis=0, keepdims=True)
+        squares = jnp.sum(fresh * fresh, axis=0, keepdims=True)
+        which = lax.broadcasted_iota(jnp.int32, (8, channels), 0)
+        stat_out[k, span] = jnp.where(which == 0, total, jnp.where(which == 1, squares, 0.0))
+
+    def edge_copy(k, side):
+        target = jnp.where(side == 0, me - 1, me + 1)
+        return pltpu.make_async_remote_copy(
+            edge_out.at[k, side], edge_in.at[k, 1 - side],
+            e_send.at[k, side], e_recv.at[k, 1 - side],
+            device_id=member(target), device_id_type=MESH,
+        )
+
+    def edge_wait(k, side):
+        return pltpu.make_async_remote_copy(
+            edge_out.at[k, side], edge_in.at[k, side],
+            e_send.at[k, side], e_recv.at[k, side],
+            device_id=member(jnp.where(side == 0, me - 1, me + 1)), device_id_type=MESH,
+        )
+
+    has = (me > 0, me < group - 1)
+
+    def stat_copy(k, c, slot):
+        return pltpu.make_async_remote_copy(
+            stat_out.at[k], stat_in.at[k, slot], s_send.at[k, c], s_recv.at[k, slot],
+            device_id=member(c), device_id_type=MESH,
+        )
+
+    def publish(k):
+        for side, column in ((0, 0), (1, TILE - 1)):
+            edge_out[k, side] = raw[pl.ds(column, lines, stride=TILE), :].astype(jnp.bfloat16)
+        for c in partners:
+            stat_copy(k, c, me).start()
+        for side in (0, 1):
+
+            @pl.when(has[side])
+            def _():
+                edge_copy(k, side).start()
+
+        stat_in[k, me] = stat_out[k]
+
+    def group_sum(t):
+        lane = lax.broadcasted_iota(jnp.int32, t.shape, 1)
+        width = t.shape[1]
+        size = 1
+        while size < width // GROUPS:
+            up = pltpu.roll(t, width - size, 1)
+            down = pltpu.roll(t, size, 1)
+            t = t + jnp.where(lax.rem(lane // size, 2) == 0, up, down)
+            size *= 2
+        return t
+
+    members = frames_here * height * TILE * group * (channels // GROUPS)
+
+    def normalize_span(k, span):
+        block = k // 2
+        which = lax.rem(k, 2)
+        total = stat_in[k, 0, span]
+        for c in range(1, group):
+            total = total + stat_in[k, c, span]
+        total = group_sum(total)
+        average = total[0:1] / members
+        squares = total[1:2] / members
+        inverse = lax.rsqrt(squares - average * average + EPS)
+        params = gbuf[block]
+        gain = jnp.where(which == 0, params[0:1], params[2:3])
+        bias = jnp.where(which == 0, params[1:2], params[3:4])
+        scale = inverse * gain
+
+        def active(u):
+            y = (u - average) * scale + bias
+            return 0.5 * y * (1.0 + jnp.tanh(0.5 * y))
+
+        count = frames_here * height
+        flat = padded.reshape(lines * 2 * TILE, channels)
+        for side, column in ((0, 7), (1, 8 + TILE)):
+
+            @pl.when(has[side])
+            def _():
+                u = edge_in[k, side, pl.ds(span * count, count)].astype(jnp.float32)
+                flat[pl.ds(span * count * 2 * TILE + column, count, stride=2 * TILE), :] = active(u)
+
+        for f in range(frames_here):
+            frame = span * frames_here + f
+            u = raw[pl.ds(frame * height * TILE, height * TILE)]
+            here = pl.ds(frame * height, height)
+            y = active(u).reshape(height, TILE, channels)
+            padded[here, 8 : 8 + TILE] = y
+            for dx in range(3):
+                shifted = y if dx == 1 else padded[here, 7 + dx : 7 + dx + TILE]
+                act[frame + 2, 1 : height + 1, :, dx * channels : (dx + 1) * channels] = (
+                    shifted.astype(jnp.bfloat16)
+                )
+
+    def convolve_span(k, span):
+        total = None
+        for dt in range(3):
+            columns = [
+                act[pl.ds(span * frames_here + dt, frames_here), dy : dy + height].reshape(
+                    span_size, 3 * channels
+                )
+                for dy in range(3)
+            ]
+            x = jnp.concatenate(columns, axis=1)
+            w = wbuf[k, dt * (taps // 3) : (dt + 1) * (taps // 3)]
+            part = jnp.dot(x, w, preferred_element_type=jnp.float32)
+            total = part if total is None else total + part
+        return total
+
+    def phase(k):
+        publish(k)
+
+        @pl.when(k <= 2)
+        def _():
+            pump(k)
+
+        @pl.when(jnp.logical_and(k >= 2, k + 1 < convs))
+        def _():
+            pump(k + 1)
+
+        for c in partners:
+            stat_copy(k, c, c).wait_recv()
+        for side in (0, 1):
+
+            @pl.when(has[side])
+            def _():
+                edge_wait(k, side).wait_recv()
+
+        for span in range(cores):
+            normalize_span(k, span)
+        arrive(k)
+
+    for c in partners:
+        src, dst = input_copy(me, c)
+        pltpu.make_async_remote_copy(
+            src, dst, in_send.at[c], in_recv.at[c], device_id=member(c), device_id_type=MESH
+        ).wait_recv()
+    own.wait()
+    for span in range(cores):
+        fresh = vin[span * frames_here : (span + 1) * frames_here]
+        fresh = fresh.reshape(span_size, channels).astype(jnp.float32)
+        values[span * span_size : (span + 1) * span_size] = fresh
+        put(0, span, fresh)
+    for s in others:
+        pltpu.make_async_remote_copy(
+            small, gbuf.at[s], g_send.at[s], g_recv.at[s],
+            device_id={"segment": s}, device_id_type=MESH,
+        ).wait_recv()
+
+    @pl.loop(0, segments)
+    def _(block):
+        k = 2 * block
+        phase(k)
+
+        @pl.loop(0, cores)
+        def _(span):
+            hidden = convolve_span(k, span)
+            put(k + 1, span, hidden.astype(jnp.bfloat16).astype(jnp.float32))
+
+        phase(k + 1)
+
+        @pl.loop(0, cores)
+        def _(span):
+            here = pl.ds(span * span_size, span_size)
+            fresh = values[here] + convolve_span(k + 1, span)
+            fresh = fresh.astype(jnp.bfloat16)
+            values[here] = fresh.astype(jnp.float32)
+            vin[pl.ds(span * frames_here, frames_here)] = fresh.reshape(
+                frames_here, height, TILE, channels
+            )
+            put(k + 2, span, fresh.astype(jnp.float32))
+
+    def output_copy(c, sender):
+        src = vin.at[
+            pl.ds(lax.rem(c, cores) * frames_here, frames_here),
+            pl.ds((c // cores) * rows_here, rows_here),
+        ]
+        return src, out.at[:, :, pl.ds(sender * TILE, TILE)]
+
+    for c in partners:
+        src, dst = output_copy(c, me)
+        pltpu.make_async_remote_copy(
+            src, dst, o_send.at[c], o_recv.at[me], device_id=member(c), device_id_type=MESH
+        ).start()
+    src, dst = output_copy(me, me)
+    own = pltpu.make_async_copy(src, dst, own_sem)
+    own.start()
+
+    for c in partners:
+        src, dst = input_copy(c, me)
+        pltpu.make_async_remote_copy(
+            src, dst, in_send.at[c], in_recv.at[me], device_id=member(c), device_id_type=MESH
+        ).wait_send()
+    for s in others:
+        pltpu.make_async_remote_copy(
+            small, gbuf.at[seg], g_send.at[s], g_recv.at[seg],
+            device_id={"segment": s}, device_id_type=MESH,
+        ).wait_send()
+    for i, source in enumerate((first, second)):
+        k = 2 * seg + i
+        for q in range(PIECES):
+            rows = pl.ds(core * half + q * piece, piece)
+            for slot, target in enumerate((across, along)):
+                pltpu.make_async_remote_copy(
+                    source.at[rows], wbuf.at[k, rows],
+                    w_send.at[k, q, slot], w_recv.at[k, core, q],
+                    device_id={"segment": target}, device_id_type=MESH,
+                ).wait_send()
+
+    @pl.loop(0, convs)
+    def _(k):
+        kind = relation(k)
+        for q in range(PIECES):
+
+            @pl.when(kind != 0)
+            def _():
+                landed(k, core, q).wait_send()
+
+            @pl.when(kind == core + 1)
+            def _():
+                forwarded(k, q).wait_send()
+
+        for c in partners:
+            stat_copy(k, c, me).wait_send()
+        for side in (0, 1):
+
+            @pl.when(has[side])
+            def _():
+                edge_copy(k, side).wait_send()
+
+    own.wait()
+    for c in partners:
+        src, dst = output_copy(me, c)
+        copy = pltpu.make_async_remote_copy(
+            src, dst, o_send.at[c], o_recv.at[c], device_id=member(c), device_id_type=MESH
+        )
+        copy.wait_recv()
+        src, dst = output_copy(c, me)
+        pltpu.make_async_remote_copy(
+            src, dst, o_send.at[c], o_recv.at[me], device_id=member(c), device_id_type=MESH
+        ).wait_send()
+
+
+def in_one_kernel(
+    latents, conv_first, conv_second, gain_first, bias_first, gain_second, bias_second
+):
+    segments = lax.axis_size("segment")
+    cores = lax.axis_size("tm")
+    group = lax.axis_size("rows") * cores
+    micro, frames_here, rows_here, columns, channels = latents.shape
+    frames, height = frames_here * cores, rows_here * lax.axis_size("rows")
+    lines, pixels = frames * height, frames * height * TILE
+    convs = 2 * segments
+    taps = 27 * channels
+    small = jnp.concatenate([gain_first, bias_first, gain_second, bias_second])
+    small = jnp.pad(small.astype(jnp.float32), ((0, 4), (0, 0)))
+    dma = pltpu.SemaphoreType.DMA
+    any_space = pl.BlockSpec(memory_space=pl.ANY)
+    vmem = pl.BlockSpec(memory_space=pltpu.VMEM)
+    result = pl.pallas_call(
+        fused,
+        out_shape=jax.ShapeDtypeStruct((frames_here, rows_here, columns, channels), jnp.bfloat16),
+        in_specs=[any_space] * 3 + [vmem],
+        out_specs=any_space,
+        scratch_shapes=[
+            pltpu.VMEM((convs, taps, channels), jnp.bfloat16),
+            pltpu.VMEM((segments, 8, channels), jnp.float32),
+            pltpu.VMEM((frames, height, TILE, channels), jnp.bfloat16),
+            pltpu.VMEM((pixels, channels), jnp.float32),
+            pltpu.VMEM((pixels, channels), jnp.float32),
+            pltpu.VMEM((lines, 2 * TILE, channels), jnp.float32),
+            pltpu.VMEM((frames + 2, height + 2, TILE, 3 * channels), jnp.bfloat16),
+            pltpu.VMEM((convs, 2, lines, channels), jnp.bfloat16),
+            pltpu.VMEM((convs, 2, lines, channels), jnp.bfloat16),
+            pltpu.VMEM((convs + 1, cores, 8, channels), jnp.float32),
+            pltpu.VMEM((convs, group, cores, 8, channels), jnp.float32),
+            dma((group,)), dma((group,)), dma,
+            dma((convs, PIECES, 3)), dma((convs, 2, PIECES)), dma((2,)),
+            dma((segments,)), dma((segments,)),
+            dma((convs, 2)), dma((convs, 2)),
+            dma((convs, group)), dma((convs, group)),
+            dma((group,)), dma((group,)),
+        ],
+        compiler_params=pltpu.CompilerParams(
+            collective_id=0, has_side_effects=True, vmem_limit_bytes=40 * 1024 * 1024
+        ),
+        cost_estimate=pl.CostEstimate(
+            flops=2 * convs * pixels * taps * channels,
+            bytes_accessed=6 * taps * channels,
+            transcendentals=convs * pixels * channels,
+        ),
+    )(latents, conv_first.reshape(taps, channels), conv_second.reshape(taps, channels), small)
+    return result[None]
+
+
+def choose(latents, *params):
+    cores = lax.axis_size("tm")
+    group = lax.axis_size("rows") * cores
+    fits = (
+        lax.axis_size("segment") == 4
+        and latents.shape[0] == 4
+        and cores == 2
+        and latents.shape[3] == group * TILE
+    )
+    return in_one_kernel(latents, *params) if fits else body(latents, *params)
+
+
 def solution(mesh):
     in_specs = (
         P(None, "tm", "rows", None, None),
@@ -104,4 +553,4 @@
         P("segment", None),
     )
     out_specs = P("segment", "tm", "rows", None, None)
-    return jax.shard_map(body, mesh=mesh, in_specs=in_specs, out_specs=out_specs, check_vma=False)
+    return jax.shard_map(choose, mesh=mesh, in_specs=in_specs, out_specs=out_specs, check_vma=False)

time: 297 us -> 106 us (0.36)
  waiting for transfers between devices: 120 us -> 0 us
  Pallas kernels: 0 us -> 100 us
  blocking collectives: 71.5 us -> 0 us
  starting transfers between devices: 41.5 us -> 0 us
  matrix products: 26.5 us -> 0 us
  between operations: 14.5 us -> 0.03 us
  local copies, waits for them, and re-layouts: 13.6 us -> 4.95 us
  other arithmetic: 7.41 us -> 0.01 us
    pallas_call x0 -> x1, Pallas kernels: none -> 100 us  [in_one_kernel(): pl.pallas_call(fused, out_shape=jax.ShapeDtypeStruct((frames_here, rows_h...]
    ppermute x24 -> x0, waiting for transfers between devices: 84.8 us -> none  [the longest x8 31.2 us: passed_along(): lax.ppermute(value, axis, [(source, source + steps) for source in range(i...]
    psum x8 -> x0, blocking collectives: 64.8 us -> none  [normalize(): lax.psum((jnp.sum(grouped, axis=(0, 1, 2, 4)), jnp.sum(grouped * grouped,...]
    ppermute x24 -> x0, starting transfers between devices: 41.4 us -> none  [the longest x8 20.3 us: padded_2(): lax.ppermute(lax.slice_in_dim(block, block.shape[dim] - width, None, axis...]
    all_gather x2 -> x0, waiting for transfers between devices: 34 us -> none  [the longest x1 19.2 us: body(): second = lax.all_gather(conv_second, 'segment', axis=0, tiled=True)]
    conv_general_dilated x8 -> x0, matrix products: 26.5 us -> none  [convolve(): lax.conv_general_dilated(padded[None], kernel, (1, 1, 1), 'VALID', dimens...]
    all_gather x1 -> x0, blocking collectives: 6.74 us -> none  [body(): small = lax.all_gather(small, 'segment', axis=0, tiled=True)]
  transfers between devices with their start and end apart: 26 -> 0, of which waited for: 26 -> 0; matrix products, arithmetic and copies ran while one was open for 3% -> 0% of each run, Pallas kernels for 0% -> 0%
where the time goes in v1:
time: 106 us; the launch traced here: 105 us
  Pallas kernels  100 us (94%)
  local copies, waits for them, and re-layouts  4.95 us (5%)
    pallas_call x1, Pallas kernels, in_one_kernel(): pl.pallas_call(fused, out_shape=jax.ShapeDtypeStruct((frames_here, rows_h...  100 us
    unnamed x15, local copies, waits for them, and re-layouts  4.95 us

profile of v1, /device:TPU:1, one launch (start us, length us, event | category | flops | bytes accessed | tf_op | source)
XLA Modules:
  0.0 105.4 jit_solution(3708471793508355374)
XLA Ops:
  0.0 0.0 copy-start.6
  0.0 0.0 copy-start.3
  0.0 0.0 copy-start.4
  0.0 0.0 copy-start.5
  0.0 0.6 copy-done.6
  0.7 0.0 copy-done.3
  0.7 0.0 copy-done.4
  0.7 0.0 copy-done.5
  0.7 0.0 copy-start
  0.7 1.2 %copy-done = bf16[4,4,2,128,128]{4,3,2,1,0:T(8,128)(2,1)S(1)} copy-done((bf16[4,4,2,128,128]{4,3,2,1,0:T(8,128)(2,1)S(1)}, bf16[4,4,2,128,128]{4,3,2,1,0:T(8,128)(2,1)}, u32[]{:S(2)}) %copy-start) | copy-done | bytes 1048600
  1.9 0.0 copy-start.1
  1.9 1.2 %copy-done.1 = bf16[1,3,3,3,128,128]{5,4,3,2,1,0:T(8,128)(2,1)S(1)} copy-done((bf16[1,3,3,3,128,128]{5,4,3,2,1,0:T(8,128)(2,1)S(1)}, bf16[1,3,3,3,128,128]{5,4,3,2,1,0:T(8,128)(2,1)}, u32[]{:S(2)}) %copy-start.1) | copy-done | bytes 884760
  3.1 0.0 copy-start.2
  3.1 1.2 %copy-done.2 = bf16[1,3,3,3,128,128]{5,4,3,2,1,0:T(8,128)(2,1)S(1)} copy-done((bf16[1,3,3,3,128,128]{5,4,3,2,1,0:T(8,128)(2,1)S(1)}, bf16[1,3,3,3,128,128]{5,4,3,2,1,0:T(8,128)(2,1)}, u32[]{:S(2)}) %copy-start.2) | copy-done | bytes 884760
  4.3 100.4 %shard_map.73 = bf16[4,2,128,128]{3,2,1,0:T(8,128)(2,1)S(1)} custom-call(bf16[4,4,2,128,128]{4,3,2,1,0:T(8,128)(2,1)S(1)} %copy-done, bf16[3456,128]{1,0:T(8,128)(2,1)S(1)} %bitcast.4, bf16[3456,128]{1,0:T(8,128)(2,1)S(1)} %bitcast.5, f32[8,128]{1,0:T(8,128)S(1)} %fusion.7.small), custom_call_target="tpu_custom_call" | custom-call | flops 7247757312 | bytes 2654208 | tf_op jit(solution)/shard_map/pallas_call | solution.py:497
  104.7 0.7 copy.9
  (1 shorter events, 0.0 us)
Async XLA Ops:
  0.0 0.7 copy-start.6
  0.0 0.7 copy-start.3
  0.0 0.7 copy-start.4
  0.0 0.7 copy-start.5
  0.7 1.2 %copy-start = (bf16[4,4,2,128,128]{4,3,2,1,0:T(8,128)(2,1)S(1)}, bf16[4,4,2,128,128]{4,3,2,1,0:T(8,128)(2,1)}, u32[]{:S(2)}) copy-start(bf16[4,4,2,128,128]{4,3,2,1,0:T(8,128)(2,1)} %latents.1) | copy-start | bytes 3145732
  1.9 1.2 %copy-start.1 = (bf16[1,3,3,3,128,128]{5,4,3,2,1,0:T(8,128)(2,1)S(1)}, bf16[1,3,3,3,128,128]{5,4,3,2,1,0:T(8,128)(2,1)}, u32[]{:S(2)}) copy-start(bf16[1,3,3,3,128,128]{5,4,3,2,1,0:T(8,128)(2,1)} %param.8) | copy-start | bytes 2654212
  3.1 1.2 %copy-start.2 = (bf16[1,3,3,3,128,128]{5,4,3,2,1,0:T(8,128)(2,1)S(1)}, bf16[1,3,3,3,128,128]{5,4,3,2,1,0:T(8,128)(2,1)}, u32[]{:S(2)}) copy-start(bf16[1,3,3,3,128,128]{5,4,3,2,1,0:T(8,128)(2,1)} %param.9) | copy-start | bytes 2654212

commit v2 on v1

--- a/solution.py
+++ b/solution.py
@@ -99,7 +99,7 @@
 
 MESH = pl.DeviceIdType.MESH
 TILE = 16
-PIECES = 2
+PIECES = 3
 
 
 def fused(
@@ -131,7 +131,8 @@
     def member(c):
         return {"rows": c // cores, "tm": lax.rem(c, cores)}
 
-    partners = [lax.rem(me + d, group) for d in range(1, group)]
+    order = sorted(range(1, group), key=lambda d: -min(d, group - d))
+    partners = [lax.rem(me + d, group) for d in order]
     others = [lax.rem(seg + d, segments) for d in range(1, segments)]
 
     barrier = pltpu.get_barrier_semaphore()
@@ -237,44 +238,47 @@
         raw[pl.ds(span * span_size, span_size)] = fresh
         total = jnp.sum(fresh, axis=0, keepdims=True)
         squares = jnp.sum(fresh * fresh, axis=0, keepdims=True)
-        which = lax.broadcasted_iota(jnp.int32, (8, channels), 0)
-        stat_out[k, span] = jnp.where(which == 0, total, jnp.where(which == 1, squares, 0.0))
-
-    def edge_copy(k, side):
-        target = jnp.where(side == 0, me - 1, me + 1)
+        stat_out[k, span] = jnp.concatenate([total, squares], axis=0)
+
+    count = frames_here * height
+
+    def edge_copy(k, side, span, landing):
         return pltpu.make_async_remote_copy(
-            edge_out.at[k, side], edge_in.at[k, 1 - side],
-            e_send.at[k, side], e_recv.at[k, 1 - side],
-            device_id=member(target), device_id_type=MESH,
+            edge_out.at[k, side, span], edge_in.at[k, landing, span],
+            e_send.at[k, side, span], e_recv.at[k, landing, span],
+            device_id=member(me - 1 if side == 0 else me + 1), device_id_type=MESH,
         )
 
-    def edge_wait(k, side):
+    has = (me > 0, me < group - 1)
+
+    def stat_copy(k, span, c, slot):
         return pltpu.make_async_remote_copy(
-            edge_out.at[k, side], edge_in.at[k, side],
-            e_send.at[k, side], e_recv.at[k, side],
-            device_id=member(jnp.where(side == 0, me - 1, me + 1)), device_id_type=MESH,
-        )
-
-    has = (me > 0, me < group - 1)
-
-    def stat_copy(k, c, slot):
-        return pltpu.make_async_remote_copy(
-            stat_out.at[k], stat_in.at[k, slot], s_send.at[k, c], s_recv.at[k, slot],
+            stat_out.at[k, span], stat_in.at[k, slot, span],
+            s_send.at[k, c, span], s_recv.at[k, slot, span],
             device_id=member(c), device_id_type=MESH,
         )
 
-    def publish(k):
+    def publish(k, span):
+        for c in partners:
+            stat_copy(k, span, c, me).start()
         for side, column in ((0, 0), (1, TILE - 1)):
-            edge_out[k, side] = raw[pl.ds(column, lines, stride=TILE), :].astype(jnp.bfloat16)
+            picked = raw[pl.ds(span * span_size + column, count, stride=TILE), :]
+            edge_out[k, side, span] = picked.astype(jnp.bfloat16)
+
+            @pl.when(has[side])
+            def _():
+                edge_copy(k, side, span, 1 - side).start()
+
+        stat_in[k, me, span] = stat_out[k, span]
+
+    def receive(k, span):
         for c in partners:
-            stat_copy(k, c, me).start()
+            stat_copy(k, span, c, c).wait_recv()
         for side in (0, 1):
 
             @pl.when(has[side])
             def _():
-                edge_copy(k, side).start()
-
-        stat_in[k, me] = stat_out[k]
+                edge_copy(k, side, span, side).wait_recv()
 
     def group_sum(t):
         lane = lax.broadcasted_iota(jnp.int32, t.shape, 1)
@@ -295,7 +299,7 @@
         total = stat_in[k, 0, span]
         for c in range(1, group):
             total = total + stat_in[k, c, span]
-        total = group_sum(total)
+        total = group_sum(jnp.concatenate([total] * 4, axis=0))
         average = total[0:1] / members
         squares = total[1:2] / members
         inverse = lax.rsqrt(squares - average * average + EPS)
@@ -308,13 +312,12 @@
             y = (u - average) * scale + bias
             return 0.5 * y * (1.0 + jnp.tanh(0.5 * y))
 
-        count = frames_here * height
         flat = padded.reshape(lines * 2 * TILE, channels)
         for side, column in ((0, 7), (1, 8 + TILE)):
 
             @pl.when(has[side])
             def _():
-                u = edge_in[k, side, pl.ds(span * count, count)].astype(jnp.float32)
+                u = edge_in[k, side, span].astype(jnp.float32)
                 flat[pl.ds(span * count * 2 * TILE + column, count, stride=2 * TILE), :] = active(u)
 
         for f in range(frames_here):
@@ -344,9 +347,7 @@
             total = part if total is None else total + part
         return total
 
-    def phase(k):
-        publish(k)
-
+    def feed(k):
         @pl.when(k <= 2)
         def _():
             pump(k)
@@ -355,17 +356,27 @@
         def _():
             pump(k + 1)
 
+    def output_copy(c, sender, span):
+        src = vin.at[
+            pl.ds(span * frames_here, frames_here), pl.ds((c // cores) * rows_here, rows_here)
+        ]
+        return src, out.at[:, :, pl.ds(sender * TILE, TILE)]
+
+    def finish(span):
         for c in partners:
-            stat_copy(k, c, c).wait_recv()
-        for side in (0, 1):
-
-            @pl.when(has[side])
-            def _():
-                edge_wait(k, side).wait_recv()
-
-        for span in range(cores):
-            normalize_span(k, span)
-        arrive(k)
+
+            @pl.when(lax.rem(c, cores) == span)
+            def _():
+                src, dst = output_copy(c, me, span)
+                pltpu.make_async_remote_copy(
+                    src, dst, o_send.at[c], o_recv.at[me],
+                    device_id=member(c), device_id_type=MESH,
+                ).start()
+
+        @pl.when(core == span)
+        def _():
+            src, dst = output_copy(me, me, span)
+            pltpu.make_async_copy(src, dst, own_sem).start()
 
     for c in partners:
         src, dst = input_copy(me, c)
@@ -378,6 +389,7 @@
         fresh = fresh.reshape(span_size, channels).astype(jnp.float32)
         values[span * span_size : (span + 1) * span_size] = fresh
         put(0, span, fresh)
+        publish(0, span)
     for s in others:
         pltpu.make_async_remote_copy(
             small, gbuf.at[s], g_send.at[s], g_recv.at[s],
@@ -387,17 +399,21 @@
     @pl.loop(0, segments)
     def _(block):
         k = 2 * block
-        phase(k)
-
-        @pl.loop(0, cores)
-        def _(span):
+        feed(k)
+        for span in range(cores):
+            receive(k, span)
+            normalize_span(k, span)
+            if span == 0:
+                arrive(k)
             hidden = convolve_span(k, span)
             put(k + 1, span, hidden.astype(jnp.bfloat16).astype(jnp.float32))
-
-        phase(k + 1)
-
-        @pl.loop(0, cores)
-        def _(span):
+            publish(k + 1, span)
+        feed(k + 1)
+        for span in range(cores):
+            receive(k + 1, span)
+            normalize_span(k + 1, span)
+            if span == 0:
+                arrive(k + 1)
             here = pl.ds(span * span_size, span_size)
             fresh = values[here] + convolve_span(k + 1, span)
             fresh = fresh.astype(jnp.bfloat16)
@@ -405,23 +421,15 @@
             vin[pl.ds(span * frames_here, frames_here)] = fresh.reshape(
                 frames_here, height, TILE, channels
             )
-            put(k + 2, span, fresh.astype(jnp.float32))
-
-    def output_copy(c, sender):
-        src = vin.at[
-            pl.ds(lax.rem(c, cores) * frames_here, frames_here),
-            pl.ds((c // cores) * rows_here, rows_here),
-        ]
-        return src, out.at[:, :, pl.ds(sender * TILE, TILE)]
-
-    for c in partners:
-        src, dst = output_copy(c, me)
-        pltpu.make_async_remote_copy(
-            src, dst, o_send.at[c], o_recv.at[me], device_id=member(c), device_id_type=MESH
-        ).start()
-    src, dst = output_copy(me, me)
-    own = pltpu.make_async_copy(src, dst, own_sem)
-    own.start()
+
+            @pl.when(block < segments - 1)
+            def _():
+                put(k + 2, span, values[here])
+                publish(k + 2, span)
+
+            @pl.when(block == segments - 1)
+            def _():
+                finish(span)
 
     for c in partners:
         src, dst = input_copy(c, me)
@@ -457,22 +465,23 @@
             def _():
                 forwarded(k, q).wait_send()
 
-        for c in partners:
-            stat_copy(k, c, me).wait_send()
-        for side in (0, 1):
-
-            @pl.when(has[side])
-            def _():
-                edge_copy(k, side).wait_send()
-
-    own.wait()
+        for span in range(cores):
+            for c in partners:
+                stat_copy(k, span, c, me).wait_send()
+            for side in (0, 1):
+
+                @pl.when(has[side])
+                def _():
+                    edge_copy(k, side, span, 1 - side).wait_send()
+
+    src, dst = output_copy(me, me, core)
+    pltpu.make_async_copy(src, dst, own_sem).wait()
     for c in partners:
-        src, dst = output_copy(me, c)
-        copy = pltpu.make_async_remote_copy(
+        src, dst = output_copy(me, c, core)
+        pltpu.make_async_remote_copy(
             src, dst, o_send.at[c], o_recv.at[c], device_id=member(c), device_id_type=MESH
-        )
-        copy.wait_recv()
-        src, dst = output_copy(c, me)
+        ).wait_recv()
+        src, dst = output_copy(c, me, lax.rem(c, cores))
         pltpu.make_async_remote_copy(
             src, dst, o_send.at[c], o_recv.at[me], device_id=member(c), device_id_type=MESH
         ).wait_send()
@@ -507,15 +516,15 @@
             pltpu.VMEM((pixels, channels), jnp.float32),
             pltpu.VMEM((lines, 2 * TILE, channels), jnp.float32),
             pltpu.VMEM((frames + 2, height + 2, TILE, 3 * channels), jnp.bfloat16),
-            pltpu.VMEM((convs, 2, lines, channels), jnp.bfloat16),
-            pltpu.VMEM((convs, 2, lines, channels), jnp.bfloat16),
-            pltpu.VMEM((convs + 1, cores, 8, channels), jnp.float32),
-            pltpu.VMEM((convs, group, cores, 8, channels), jnp.float32),
+            pltpu.VMEM((convs, 2, cores, lines // cores, channels), jnp.bfloat16),
+            pltpu.VMEM((convs, 2, cores, lines // cores, channels), jnp.bfloat16),
+            pltpu.VMEM((convs, cores, 2, channels), jnp.float32),
+            pltpu.VMEM((convs, group, cores, 2, channels), jnp.float32),
             dma((group,)), dma((group,)), dma,
             dma((convs, PIECES, 3)), dma((convs, 2, PIECES)), dma((2,)),
             dma((segments,)), dma((segments,)),
-            dma((convs, 2)), dma((convs, 2)),
-            dma((convs, group)), dma((convs, group)),
+            dma((convs, 2, cores)), dma((convs, 2, cores)),
+            dma((convs, group, cores)), dma((convs, group, cores)),
             dma((group,)), dma((group,)),
         ],
         compiler_params=pltpu.CompilerParams(

time: 106 us -> 101 us (0.953)
  Pallas kernels: 100 us -> 95.4 us
    pallas_call x1, Pallas kernels: 100 us -> 95.4 us  [in_one_kernel(): pl.pallas_call(fused, out_shape=jax.ShapeDtypeStruct((frames_here, rows_h...]
where the time goes in v2:
time: 101 us; the launch traced here: 100 us
  Pallas kernels  95.4 us (94%)
  local copies, waits for them, and re-layouts  4.95 us (5%)
    pallas_call x1, Pallas kernels, in_one_kernel(): pl.pallas_call(fused, out_shape=jax.ShapeDtypeStruct((frames_here, rows_h...  95.4 us
    unnamed x15, local copies, waits for them, and re-layouts  4.95 us

profile of v2, /device:TPU:1, one launch (start us, length us, event | category | flops | bytes accessed | tf_op | source)
XLA Modules:
  0.0 100.4 jit_solution(6170199245895051506)
XLA Ops:
  0.0 0.0 copy-start.6
  0.0 0.0 copy-start.3
  0.0 0.0 copy-start.4
  0.0 0.0 copy-start.5
  0.0 0.6 copy-done.6
  0.7 0.0 copy-done.3
  0.7 0.0 copy-done.4
  0.7 0.0 copy-done.5
  0.7 0.0 copy-start
  0.7 1.2 %copy-done = bf16[4,4,2,128,128]{4,3,2,1,0:T(8,128)(2,1)S(1)} copy-done((bf16[4,4,2,128,128]{4,3,2,1,0:T(8,128)(2,1)S(1)}, bf16[4,4,2,128,128]{4,3,2,1,0:T(8,128)(2,1)}, u32[]{:S(2)}) %copy-start) | copy-done | bytes 1048600
  1.9 0.0 copy-start.1
  1.9 1.2 %copy-done.1 = bf16[1,3,3,3,128,128]{5,4,3,2,1,0:T(8,128)(2,1)S(1)} copy-done((bf16[1,3,3,3,128,128]{5,4,3,2,1,0:T(8,128)(2,1)S(1)}, bf16[1,3,3,3,128,128]{5,4,3,2,1,0:T(8,128)(2,1)}, u32[]{:S(2)}) %copy-start.1) | copy-done | bytes 884760
  3.1 0.0 copy-start.2
  3.1 1.2 %copy-done.2 = bf16[1,3,3,3,128,128]{5,4,3,2,1,0:T(8,128)(2,1)S(1)} copy-done((bf16[1,3,3,3,128,128]{5,4,3,2,1,0:T(8,128)(2,1)S(1)}, bf16[1,3,3,3,128,128]{5,4,3,2,1,0:T(8,128)(2,1)}, u32[]{:S(2)}) %copy-start.2) | copy-done | bytes 884760
  4.3 95.4 %shard_map.73 = bf16[4,2,128,128]{3,2,1,0:T(8,128)(2,1)S(1)} custom-call(bf16[4,4,2,128,128]{4,3,2,1,0:T(8,128)(2,1)S(1)} %copy-done, bf16[3456,128]{1,0:T(8,128)(2,1)S(1)} %bitcast.4, bf16[3456,128]{1,0:T(8,128)(2,1)S(1)} %bitcast.5, f32[8,128]{1,0:T(8,128)S(1)} %fusion.7.small), custom_call_target="tpu_custom_call" | custom-call | flops 7247757312 | bytes 2654208 | tf_op jit(solution)/shard_map/pallas_call | solution.py:506
  99.7 0.7 copy.9
  (1 shorter events, 0.0 us)
Async XLA Ops:
  0.0 0.7 copy-start.6
  0.0 0.7 copy-start.3
  0.0 0.7 copy-start.4
  0.0 0.7 copy-start.5
  0.7 1.2 %copy-start = (bf16[4,4,2,128,128]{4,3,2,1,0:T(8,128)(2,1)S(1)}, bf16[4,4,2,128,128]{4,3,2,1,0:T(8,128)(2,1)}, u32[]{:S(2)}) copy-start(bf16[4,4,2,128,128]{4,3,2,1,0:T(8,128)(2,1)} %latents.1) | copy-start | bytes 3145732
  1.9 1.2 %copy-start.1 = (bf16[1,3,3,3,128,128]{5,4,3,2,1,0:T(8,128)(2,1)S(1)}, bf16[1,3,3,3,128,128]{5,4,3,2,1,0:T(8,128)(2,1)}, u32[]{:S(2)}) copy-start(bf16[1,3,3,3,128,128]{5,4,3,2,1,0:T(8,128)(2,1)} %param.8) | copy-start | bytes 2654212
  3.1 1.2 %copy-start.2 = (bf16[1,3,3,3,128,128]{5,4,3,2,1,0:T(8,128)(2,1)S(1)}, bf16[1,3,3,3,128,128]{5,4,3,2,1,0:T(8,128)(2,1)}, u32[]{:S(2)}) copy-start(bf16[1,3,3,3,128,128]{5,4,3,2,1,0:T(8,128)(2,1)} %param.9) | copy-start | bytes 2654212

commit v3 on v2

--- a/solution.py
+++ b/solution.py
@@ -142,18 +142,24 @@
         pl.semaphore_signal(barrier, inc=1, device_id={"segment": s}, device_id_type=MESH)
     pl.semaphore_wait(barrier, group - 1 + segments - 1)
 
-    def start_owner(i, source):
+    def start_owner(i, slot):
         k = 2 * seg + i
         for q in range(PIECES):
             rows = pl.ds(core * half + q * piece, piece)
-            for slot, target in enumerate((across, along)):
-                pltpu.make_async_remote_copy(
-                    source.at[rows], wbuf.at[k, rows],
-                    w_send.at[k, q, slot], w_recv.at[k, core, q],
-                    device_id={"segment": target}, device_id_type=MESH,
-                ).start()
-
-    start_owner(0, first)
+            pltpu.make_async_remote_copy(
+                (first, second)[i].at[rows], wbuf.at[k, rows],
+                w_send.at[k, q, slot], w_recv.at[k, core, q],
+                device_id={"segment": (across, along)[slot]}, device_id_type=MESH,
+            ).start()
+
+    late = (seg == 2, seg == 1)
+    last = seg == segments - 1
+
+    for slot in (0, 1):
+
+        @pl.when(jnp.logical_not(late[slot]))
+        def _():
+            start_owner(0, slot)
 
     def input_copy(c, sender):
         dst = vin.at[
@@ -181,7 +187,12 @@
 
     for i, source in enumerate((first, second)):
         pltpu.make_async_copy(source, wbuf.at[2 * seg + i], w_own.at[i]).start()
-    start_owner(1, second)
+    for slot in (0, 1):
+
+        @pl.when(jnp.logical_not(jnp.logical_or(late[slot], last)))
+        def _():
+            start_owner(1, slot)
+
 
     act[...] = jnp.zeros_like(act)
     padded[...] = jnp.zeros_like(padded)
@@ -347,12 +358,32 @@
             total = part if total is None else total + part
         return total
 
+    ahead = jnp.where(core == 0, across, along)
+
     def feed(k):
-        @pl.when(k <= 2)
+        @pl.when(k <= 1)
         def _():
             pump(k)
 
-        @pl.when(jnp.logical_and(k >= 2, k + 1 < convs))
+        for slot in (0, 1):
+
+            @pl.when(jnp.logical_and(k == 0, late[slot]))
+            def _():
+                start_owner(0, slot)
+
+            @pl.when(jnp.logical_and(k == 1, jnp.logical_or(late[slot], last)))
+            def _():
+                start_owner(1, slot)
+
+        @pl.when(jnp.logical_and(jnp.logical_or(k == 1, k == 2), ahead != 0))
+        def _():
+            pump(2 * ahead + k - 1)
+
+        @pl.when(jnp.logical_and(k == 2, ahead != 1))
+        def _():
+            pump(k)
+
+        @pl.when(jnp.logical_and(jnp.logical_and(k >= 2, k + 1 < convs), (k + 1) // 2 != ahead))
         def _():
             pump(k + 1)
 

time: 101 us -> 105 us (1.040)
  the two profiles are of different devices: /device:TPU:1 before, /device:TPU:5 now
where the time goes in v3:
time: 105 us
  Pallas kernels  100 us (95%)
  local copies, waits for them, and re-layouts  4.95 us (5%)
    pallas_call x1, Pallas kernels, in_one_kernel(): pl.pallas_call(fused, out_shape=jax.ShapeDtypeStruct((frames_here, rows_h...  100 us
    unnamed x15, local copies, waits for them, and re-layouts  4.95 us

profile of v3, /device:TPU:5, one launch (start us, length us, event | category | flops | bytes accessed | tf_op | source)
XLA Modules:
  0.0 105.1 jit_solution(17295695402903826416)
XLA Ops:
  0.0 0.0 copy-start.6
  0.0 0.0 copy-start.3
  0.0 0.0 copy-start.4
  0.0 0.0 copy-start.5
  0.0 0.6 copy-done.6
  0.7 0.0 copy-done.3
  0.7 0.0 copy-done.4
  0.7 0.0 copy-done.5
  0.7 0.0 copy-start
  0.7 1.2 %copy-done = bf16[4,4,2,128,128]{4,3,2,1,0:T(8,128)(2,1)S(1)} copy-done((bf16[4,4,2,128,128]{4,3,2,1,0:T(8,128)(2,1)S(1)}, bf16[4,4,2,128,128]{4,3,2,1,0:T(8,128)(2,1)}, u32[]{:S(2)}) %copy-start) | copy-done | bytes 1048600
  1.9 0.0 copy-start.1
  1.9 1.2 %copy-done.1 = bf16[1,3,3,3,128,128]{5,4,3,2,1,0:T(8,128)(2,1)S(1)} copy-done((bf16[1,3,3,3,128,128]{5,4,3,2,1,0:T(8,128)(2,1)S(1)}, bf16[1,3,3,3,128,128]{5,4,3,2,1,0:T(8,128)(2,1)}, u32[]{:S(2)}) %copy-start.1) | copy-done | bytes 884760
  3.1 0.0 copy-start.2
  3.1 1.2 %copy-done.2 = bf16[1,3,3,3,128,128]{5,4,3,2,1,0:T(8,128)(2,1)S(1)} copy-done((bf16[1,3,3,3,128,128]{5,4,3,2,1,0:T(8,128)(2,1)S(1)}, bf16[1,3,3,3,128,128]{5,4,3,2,1,0:T(8,128)(2,1)}, u32[]{:S(2)}) %copy-start.2) | copy-done | bytes 884760
  4.3 100.2 %shard_map.73 = bf16[4,2,128,128]{3,2,1,0:T(8,128)(2,1)S(1)} custom-call(bf16[4,4,2,128,128]{4,3,2,1,0:T(8,128)(2,1)S(1)} %copy-done, bf16[3456,128]{1,0:T(8,128)(2,1)S(1)} %bitcast.4, bf16[3456,128]{1,0:T(8,128)(2,1)S(1)} %bitcast.5, f32[8,128]{1,0:T(8,128)S(1)} %fusion.7.small), custom_call_target="tpu_custom_call" | custom-call | flops 7247757312 | bytes 2654208 | tf_op jit(solution)/shard_map/pallas_call | solution.py:537
  104.4 0.7 copy.9
  (1 shorter events, 0.0 us)
Async XLA Ops:
  0.0 0.7 copy-start.6
  0.0 0.7 copy-start.3
  0.0 0.7 copy-start.4
  0.0 0.7 copy-start.5
  0.7 1.2 %copy-start = (bf16[4,4,2,128,128]{4,3,2,1,0:T(8,128)(2,1)S(1)}, bf16[4,4,2,128,128]{4,3,2,1,0:T(8,128)(2,1)}, u32[]{:S(2)}) copy-start(bf16[4,4,2,128,128]{4,3,2,1,0:T(8,128)(2,1)} %latents.1) | copy-start | bytes 3145732
  1.9 1.2 %copy-start.1 = (bf16[1,3,3,3,128,128]{5,4,3,2,1,0:T(8,128)(2,1)S(1)}, bf16[1,3,3,3,128,128]{5,4,3,2,1,0:T(8,128)(2,1)}, u32[]{:S(2)}) copy-start(bf16[1,3,3,3,128,128]{5,4,3,2,1,0:T(8,128)(2,1)} %param.8) | copy-start | bytes 2654212
  3.1 1.2 %copy-start.2 = (bf16[1,3,3,3,128,128]{5,4,3,2,1,0:T(8,128)(2,1)S(1)}, bf16[1,3,3,3,128,128]{5,4,3,2,1,0:T(8,128)(2,1)}, u32[]{:S(2)}) copy-start(bf16[1,3,3,3,128,128]{5,4,3,2,1,0:T(8,128)(2,1)} %param.9) | copy-start | bytes 2654212

commit v4 on v3

--- a/solution.py
+++ b/solution.py
@@ -152,14 +152,8 @@
                 device_id={"segment": (across, along)[slot]}, device_id_type=MESH,
             ).start()
 
-    late = (seg == 2, seg == 1)
-    last = seg == segments - 1
-
     for slot in (0, 1):
-
-        @pl.when(jnp.logical_not(late[slot]))
-        def _():
-            start_owner(0, slot)
+        start_owner(0, slot)
 
     def input_copy(c, sender):
         dst = vin.at[
@@ -188,11 +182,7 @@
     for i, source in enumerate((first, second)):
         pltpu.make_async_copy(source, wbuf.at[2 * seg + i], w_own.at[i]).start()
     for slot in (0, 1):
-
-        @pl.when(jnp.logical_not(jnp.logical_or(late[slot], last)))
-        def _():
-            start_owner(1, slot)
-
+        start_owner(1, slot)
 
     act[...] = jnp.zeros_like(act)
     padded[...] = jnp.zeros_like(padded)
@@ -364,16 +354,6 @@
         @pl.when(k <= 1)
         def _():
             pump(k)
-
-        for slot in (0, 1):
-
-            @pl.when(jnp.logical_and(k == 0, late[slot]))
-            def _():
-                start_owner(0, slot)
-
-            @pl.when(jnp.logical_and(k == 1, jnp.logical_or(late[slot], last)))
-            def _():
-                start_owner(1, slot)
 
         @pl.when(jnp.logical_and(jnp.logical_or(k == 1, k == 2), ahead != 0))
         def _():

time: 105 us -> 89 us (0.85)
  Pallas kernels: 100 us -> 83.8 us
    pallas_call x1, Pallas kernels: 100 us -> 83.8 us  [in_one_kernel(): pl.pallas_call(fused, out_shape=jax.ShapeDtypeStruct((frames_here, rows_h...]
where the time goes in v4:
time: 89 us; the launch traced here: 88.8 us
  Pallas kernels  83.8 us (94%)
  local copies, waits for them, and re-layouts  4.95 us (6%)
    pallas_call x1, Pallas kernels, in_one_kernel(): pl.pallas_call(fused, out_shape=jax.ShapeDtypeStruct((frames_here, rows_h...  83.8 us
    unnamed x15, local copies, waits for them, and re-layouts  4.95 us

profile of v4, /device:TPU:5, one launch (start us, length us, event | category | flops | bytes accessed | tf_op | source)
XLA Modules:
  0.0 88.8 jit_solution(474252964500550808)
XLA Ops:
  0.0 0.0 copy-start.6
  0.0 0.0 copy-start.3
  0.0 0.0 copy-start.4
  0.0 0.0 copy-start.5
  0.0 0.6 copy-done.6
  0.7 0.0 copy-done.3
  0.7 0.0 copy-done.4
  0.7 0.0 copy-done.5
  0.7 0.0 copy-start
  0.7 1.2 %copy-done = bf16[4,4,2,128,128]{4,3,2,1,0:T(8,128)(2,1)S(1)} copy-done((bf16[4,4,2,128,128]{4,3,2,1,0:T(8,128)(2,1)S(1)}, bf16[4,4,2,128,128]{4,3,2,1,0:T(8,128)(2,1)}, u32[]{:S(2)}) %copy-start) | copy-done | bytes 1048600
  1.9 0.0 copy-start.1
  1.9 1.2 %copy-done.1 = bf16[1,3,3,3,128,128]{5,4,3,2,1,0:T(8,128)(2,1)S(1)} copy-done((bf16[1,3,3,3,128,128]{5,4,3,2,1,0:T(8,128)(2,1)S(1)}, bf16[1,3,3,3,128,128]{5,4,3,2,1,0:T(8,128)(2,1)}, u32[]{:S(2)}) %copy-start.1) | copy-done | bytes 884760
  3.1 0.0 copy-start.2
  3.1 1.2 %copy-done.2 = bf16[1,3,3,3,128,128]{5,4,3,2,1,0:T(8,128)(2,1)S(1)} copy-done((bf16[1,3,3,3,128,128]{5,4,3,2,1,0:T(8,128)(2,1)S(1)}, bf16[1,3,3,3,128,128]{5,4,3,2,1,0:T(8,128)(2,1)}, u32[]{:S(2)}) %copy-start.2) | copy-done | bytes 884760
  4.3 83.8 %shard_map.73 = bf16[4,2,128,128]{3,2,1,0:T(8,128)(2,1)S(1)} custom-call(bf16[4,4,2,128,128]{4,3,2,1,0:T(8,128)(2,1)S(1)} %copy-done, bf16[3456,128]{1,0:T(8,128)(2,1)S(1)} %bitcast.4, bf16[3456,128]{1,0:T(8,128)(2,1)S(1)} %bitcast.5, f32[8,128]{1,0:T(8,128)S(1)} %fusion.7.small), custom_call_target="tpu_custom_call" | custom-call | flops 7247757312 | bytes 2654208 | tf_op jit(solution)/shard_map/pallas_call | solution.py:517
  88.1 0.7 copy.9
  (1 shorter events, 0.0 us)
Async XLA Ops:
  0.0 0.7 copy-start.6
  0.0 0.7 copy-start.3
  0.0 0.7 copy-start.4
  0.0 0.7 copy-start.5
  0.7 1.2 %copy-start = (bf16[4,4,2,128,128]{4,3,2,1,0:T(8,128)(2,1)S(1)}, bf16[4,4,2,128,128]{4,3,2,1,0:T(8,128)(2,1)}, u32[]{:S(2)}) copy-start(bf16[4,4,2,128,128]{4,3,2,1,0:T(8,128)(2,1)} %latents.1) | copy-start | bytes 3145732
  1.9 1.2 %copy-start.1 = (bf16[1,3,3,3,128,128]{5,4,3,2,1,0:T(8,128)(2,1)S(1)}, bf16[1,3,3,3,128,128]{5,4,3,2,1,0:T(8,128)(2,1)}, u32[]{:S(2)}) copy-start(bf16[1,3,3,3,128,128]{5,4,3,2,1,0:T(8,128)(2,1)} %param.8) | copy-start | bytes 2654212
  3.1 1.2 %copy-start.2 = (bf16[1,3,3,3,128,128]{5,4,3,2,1,0:T(8,128)(2,1)S(1)}, bf16[1,3,3,3,128,128]{5,4,3,2,1,0:T(8,128)(2,1)}, u32[]{:S(2)}) copy-start(bf16[1,3,3,3,128,128]{5,4,3,2,1,0:T(8,128)(2,1)} %param.9) | copy-start | bytes 2654212
